TPU v7x, 32 devices: a whole 2x2x4 slice. The times are simulated.
32 devices in a mesh: mem: 2 (over core), state: 16 (over z, y, x).
Axes of the slice: x: 2, y: 2, z: 4, core: 2. Of those that a mesh axis runs over, the one named last changes fastest.
Arguments:
- background_ensemble: bfloat16 [80, 1048576], P('mem', 'state'), may hold values from -6 to 6
- measured_segment_index: int32 [2, 256], replicated, may hold values from 0 to 31
- measured_place_within_segment: int32 [2, 256], replicated, may hold values from 0 to 32767
- measured_readings: float32 [2, 256], replicated, may hold values from -6 to 6
- measured_noise_spread: float32 [2, 256], replicated, may hold values from 0.25 to 4
- measured_damping_weight: float32 [2, 256], replicated, may hold values from 0.3 to 1
- measured_cutoff_extent: int32 [2, 256], replicated, may hold values from 1 to 1024
Outputs:
- analysis: bfloat16 [80, 1048576], P('mem', 'state')
Inputs may be any that keep to these rules, and one draw needn't show every extreme that they name: measured_segment_index numbers the blocks of 32768 state values in the order of the state dimension. measured_place_within_segment is a position inside the owner's block.
All inputs are finite; a program needn't handle non-finite values.
Results may differ from a plain program's by a relative error of at most 0.0051.
Values may be sent and summed in bfloat16 or wider, within the bound.
A program may use at most 64 MiB of HBM per device.

v0:
```python
import jax
import jax.numpy as jnp
from jax import lax
from jax.sharding import PartitionSpec as P

ENSEMBLE_COUNT = 80
SD = 32768
K = 256
B = 2
LB = 128
BLK = 4096


def observe_stats(prior_ens, values, variances):
    centre = jnp.mean(prior_ens, axis=0)
    anomaly = prior_ens - centre
    prior_var = jnp.sum(anomaly * anomaly, axis=0) / (ENSEMBLE_COUNT - 1) + 1e-06
    post_var = 1.0 / (1.0 / prior_var + 1.0 / variances)
    post_mean = post_var * (centre / prior_var + values / variances)
    shrink = jnp.sqrt(post_var / prior_var)
    increment = (post_mean - centre + (shrink - 1.0) * anomaly).astype(jnp.bfloat16)
    scaling = 1.0 / ((ENSEMBLE_COUNT - 1) * prior_var)
    return (increment, anomaly.astype(jnp.bfloat16), scaling)


def taper_weights(columns, obs_index, taper_row, reach_row):
    distance = jnp.abs(columns[:, None] // LB - obs_index[None, :] // LB).astype(jnp.float32)
    return taper_row[None, :] * jnp.maximum(
        0.0, 1.0 - distance / (reach_row[None, :].astype(jnp.float32) + 1.0)
    )


def update_block(
    block_values, columns, obs_index, taper_row, reach_row, increment, anomaly, scaling
):
    values = block_values.astype(jnp.float32)
    centred = (values - jnp.mean(values, axis=0)).astype(jnp.bfloat16)
    covariance = lax.dot_general(
        centred, anomaly, (((0,), (0,)), ((), ())), preferred_element_type=jnp.float32
    )
    gain_matrix = (
        taper_weights(columns, obs_index, taper_row, reach_row) * covariance * scaling[None, :]
    ).astype(jnp.bfloat16)
    change = lax.dot_general(
        increment, gain_matrix, (((1,), (1,)), ((), ())), preferred_element_type=jnp.float32
    )
    return (values + change).astype(jnp.bfloat16)


def collect_prior(realization_vectors, owner_row, local_row, my_block, col_offset):
    picked = jnp.take(realization_vectors, col_offset + local_row, axis=1).astype(jnp.float32)
    return jnp.where((owner_row == my_block)[None, :], picked, 0.0)


def apply_batch(
    realization_vectors, column_base, obs_index, taper_row, reach_row, increment, anomaly, scaling
):

    def advance(block_no, buffer):
        start_col = block_no * BLK
        block_values = lax.dynamic_slice_in_dim(buffer, start_col, BLK, 1)
        columns = column_base + start_col + jnp.arange(BLK, dtype=jnp.int32)
        renewed = update_block(
            block_values, columns, obs_index, taper_row, reach_row, increment, anomaly, scaling
        )
        return lax.dynamic_update_slice_in_dim(buffer, renewed, start_col, 1)

    return lax.fori_loop(0, realization_vectors.shape[1] // BLK, advance, realization_vectors)


def on_device(
    background_ensemble,
    measured_segment_index,
    measured_place_within_segment,
    measured_readings,
    measured_noise_spread,
    measured_damping_weight,
    measured_cutoff_extent,
):
    pieces = lax.axis_size("mem")
    member_row = lax.axis_index("mem")
    slab_index = lax.axis_index("state")
    member_count = background_ensemble.shape[0]
    my_block = slab_index * pieces + member_row
    early_prior = None
    column = (measured_segment_index[0] - slab_index * pieces) * SD + measured_place_within_segment[
        0
    ]
    is_held = measured_segment_index[0] // pieces == slab_index
    picked = jnp.take(
        background_ensemble, jnp.clip(column, 0, background_ensemble.shape[1] - 1), axis=1
    ).astype(jnp.float32)
    picked = jnp.where(is_held[None, :], picked, 0.0)
    padded = lax.dynamic_update_slice_in_dim(
        jnp.zeros((member_count * pieces, K), jnp.float32), picked, member_row * member_count, 0
    )
    early_prior = lax.psum(padded, ("mem", "state"))
    realization_vectors = lax.all_to_all(
        background_ensemble, "mem", split_axis=1, concat_axis=0, tiled=True
    )
    column_base = my_block * SD
    col_offset = 0
    for batch_no in range(B):
        if batch_no == 0 and early_prior is not None:
            prior_ens = early_prior
        else:
            prior_ens = lax.psum(
                collect_prior(
                    realization_vectors,
                    measured_segment_index[batch_no],
                    measured_place_within_segment[batch_no],
                    my_block,
                    col_offset,
                ),
                ("mem", "state"),
            )
        obs_index = measured_segment_index[batch_no] * SD + measured_place_within_segment[batch_no]
        increment, anomaly, scaling = observe_stats(
            prior_ens, measured_readings[batch_no], measured_noise_spread[batch_no]
        )
        realization_vectors = apply_batch(
            realization_vectors,
            column_base,
            obs_index,
            measured_damping_weight[batch_no],
            measured_cutoff_extent[batch_no],
            increment,
            anomaly,
            scaling,
        )
    return lax.all_to_all(realization_vectors, "mem", split_axis=0, concat_axis=1, tiled=True)


def solution(mesh):
    placed = (P("mem", "state"), P(), P(), P(), P(), P(), P())
    return jax.shard_map(
        on_device, mesh=mesh, in_specs=placed, out_specs=P("mem", "state"), check_vma=False
    )
```

profile of v0, /device:TPU:0, one launch (start us, length us, event | category | flops | bytes accessed | tf_op | source)
XLA Modules:
  0.0 388.0 jit_solution(6497974720385843042)
XLA Ops:
  6.5 0.8 compare_reduce_fusion.2
  7.3 0.8 compare_select_fusion.3
  8.1 14.3 %copy.29 = bf16[40,65536]{0,1:T(8,128)(2,1)} copy(bf16[40,65536]{1,0:T(8,128)(2,1)} %param.11) | data formatting | bytes 10485760 | tf_op args[0]
  22.4 8.7 %gather_fusion = bf16[256,40]{1,0:T(8,128)(2,1)S(1)} fusion(bf16[40,65536]{0,1:T(8,128)(2,1)} %copy.29, s32[1024]{0:T(1024)S(1)} %pad_clamp_fusion.1), kind=kCustom, calls=%fused_computation | custom fusion | bytes 41984 | tf_op jit(solution)/shard_map/jit(_take)/gather | solution.py:90
  31.1 0.1 select_bitcast_fusion.1
  31.2 0.1 copy.30
  31.3 0.6 copy-done
  31.9 0.0 all-reduce.3.cloned.1.call-update
  32.0 5.2 %copy.38 = bf16[5,2,8,32768]{3,2,0,1:T(8,128)(2,1)} copy(bf16[5,2,8,32768]{3,2,1,0:T(8,128)(2,1)} %bitcast.85) | data formatting | bytes 10485760 | tf_op jit(solution)/shard_map/all_to_all | solution.py:98
  37.2 0.0 copy-start.5
  37.2 0.0 copy-start.6
  37.2 6.2 %all-to-all-start = ((bf16[40,2,32768]{2,0,1:T(8,128)(2,1)}), bf16[40,2,32768]{2,0,1:T(8,128)(2,1)}, u32[]{:S(2)}, u32[]{:S(2)}) async-start(bf16[40,2,32768]{2,0,1:T(8,128)(2,1)} %bitcast.83), calls=%async_computation | async-start | bytes 10485760 | tf_op jit(solution)/shard_map/all_to_all | solution.py:98
  43.4 0.0 all-reduce.5.cloned.1.call-start
  43.5 111.6 %all-reduce.3.cloned.1.call-done = f32[80,256]{1,0:T(8,128)} async-done(((f32[80,256]{1,0:T(8,128)}), f32[80,256]{1,0:T(8,128)}) %all-reduce.3.cloned.1.call-update) | async-done | bytes 81936 | tf_op jit(solution)/shard_map/psum | solution.py:97
  155.1 0.9 reduce_sum.70
  156.1 0.9 multiply_reduce_fusion.1
  157.0 0.9 add_convert_fusion.1
  157.9 0.0 all-to-all-done
  158.0 33.8 %while.32 = (s32[]{:T(128)}, bf16[80,32768]{1,0:T(8,128)(2,1)}, f32[1,256]{1,0:T(1,128)S(1)}, s32[]{:T(128)}, s32[1,256]{1,0:T(1,128)S(1)}, /*index=5*/s32[256]{...) while((s32[]{:T(128)}, bf16[80,32768]{1,0:T(8,128)(2,1)}, ...), condition=%wide.region_5.6_spmd, body=%wide.region_3.5_spmd.sunk | while | flops 348720640 | bytes 3467987 | solution.py:68
  158.0 1.2 convert_reduce_fusion.4
  159.3 2.9 fusion.49
  162.2 1.2 convert_reduce_fusion.4
  163.5 2.9 fusion.49
  166.4 1.2 convert_reduce_fusion.4
  167.7 2.9 fusion.49
  170.7 1.2 convert_reduce_fusion.4
  172.0 3.0 fusion.49
  174.9 1.2 convert_reduce_fusion.4
  176.2 2.9 fusion.49
  179.1 1.2 convert_reduce_fusion.4
  180.4 2.9 fusion.49
  183.3 1.2 convert_reduce_fusion.4
  184.6 2.9 fusion.49
  187.5 1.2 convert_reduce_fusion.4
  188.8 2.9 fusion.49
  191.8 9.5 %copy.31 = bf16[80,32768]{0,1:T(8,128)(2,1)} copy(bf16[80,32768]{1,0:T(8,128)(2,1)} %get-tuple-element.860) | data formatting | bytes 10485760 | tf_op jit(solution)/shard_map/while | solution.py:68
  201.3 5.2 %gather_fusion.1 = bf16[256,80]{1,0:T(8,128)(2,1)S(1)} fusion(bf16[80,32768]{0,1:T(8,128)(2,1)} %copy.31, s32[1024]{0:T(1024)S(1)} %pad_clamp_fusion), kind=kCustom, calls=%fused_computation.1 | custom fusion | bytes 82944 | tf_op jit(solution)/shard_map/jit(_take)/gather | solution.py:51
  206.4 0.8 select_bitcast_fusion
  207.2 0.0 all-reduce.5.cloned.1.call-update
  207.3 124.5 %all-reduce.5.cloned.1.call-done = f32[80,256]{0,1:T(8,128)} async-done(((f32[80,256]{0,1:T(8,128)}), f32[80,256]{0,1:T(8,128)}) %all-reduce.5.cloned.1.call-update) | async-done | bytes 81936 | tf_op jit(solution)/shard_map/psum | solution.py:107
  331.8 1.0 reduce_sum.72
  332.8 1.1 multiply_reduce_fusion
  334.0 1.1 add_convert_fusion
  335.1 0.1 copy.32
  335.2 0.1 copy.33
  335.3 33.8 %while.33 = (s32[]{:T(128)}, bf16[80,32768]{1,0:T(8,128)(2,1)}, f32[1,256]{1,0:T(1,128)S(1)}, s32[]{:T(128)}, s32[1,256]{1,0:T(1,128)S(1)}, /*index=5*/s32[256]{...) while((s32[]{:T(128)}, bf16[80,32768]{1,0:T(8,128)(2,1)}, ...), condition=%wide.region_11.12_spmd, body=%wide.region_9.11_spmd.sunk | while | flops 348720640 | bytes 3467987 | solution.py:68
  335.3 1.2 convert_reduce_fusion.5
  336.6 2.9 fusion.53
  339.5 1.2 convert_reduce_fusion.5
  340.8 2.9 fusion.53
  343.7 1.2 convert_reduce_fusion.5
  345.0 2.9 fusion.53
  348.0 1.2 convert_reduce_fusion.5
  349.3 3.0 fusion.53
  352.2 1.2 convert_reduce_fusion.5
  353.5 2.9 fusion.53
  356.4 1.2 convert_reduce_fusion.5
  357.7 2.9 fusion.53
  360.6 1.2 convert_reduce_fusion.5
  361.9 2.9 fusion.53
  364.9 1.2 convert_reduce_fusion.5
  366.2 2.9 fusion.53
  369.1 9.4 %all_to_all.38 = bf16[2,40,32768]{2,1,0:T(8,128)(2,1)S(1)} all-to-all(bf16[2,40,32768]{2,1,0:T(8,128)(2,1)} %bitcast.28), channel_id=1, replica_groups=mesh['mem'=2,'state'=16] {'mem'}, dimensions={0} | all-to-all | bytes 10485760 | tf_op jit(solution)/shard_map/all_to_all | solution.py:131
  378.5 2.7 copy.36
  (110 shorter events, 1.1 us)
Async XLA Ops:
  6.5 148.6 %all-reduce.3.cloned.1.call-start = ((), (), s32[]{:S(2)}) async-start(), calls=%async_computation.2 | async-start | bytes 163840 | tf_op jit(solution)/shard_map/psum | solution.py:97
  31.3 0.6 copy-start
  37.2 6.3 %copy-start.1 = (s32[2,256]{1,0:T(2,128)S(1)}, s32[2,256]{1,0:T(2,128)}, u32[]{:S(2)}) copy-start(s32[2,256]{1,0:T(2,128)} %param.12) | copy-start | bytes 6148
  37.2 6.3 %copy-start.2 = (s32[2,256]{1,0:T(2,128)S(1)}, s32[2,256]{1,0:T(2,128)}, u32[]{:S(2)}) copy-start(s32[2,256]{1,0:T(2,128)} %param.13) | copy-start | bytes 6148
  37.2 6.3 %copy-start.3 = (s32[2,256]{1,0:T(2,128)S(1)}, s32[2,256]{1,0:T(2,128)}, u32[]{:S(2)}) copy-start(s32[2,256]{1,0:T(2,128)} %param.17) | copy-start | bytes 6148
  37.2 6.3 %copy-start.4 = (f32[2,256]{1,0:T(2,128)S(1)}, f32[2,256]{1,0:T(2,128)}, u32[]{:S(2)}) copy-start(f32[2,256]{1,0:T(2,128)} %param.16) | copy-start | bytes 6148
  37.2 119.8 %copy-start.5 = (f32[2,256]{1,0:T(2,128)S(1)}, f32[2,256]{1,0:T(2,128)}, u32[]{:S(2)}) copy-start(f32[2,256]{1,0:T(2,128)} %param.14) | copy-start | bytes 6148
  37.2 119.8 %copy-start.6 = (f32[2,256]{1,0:T(2,128)S(1)}, f32[2,256]{1,0:T(2,128)}, u32[]{:S(2)}) copy-start(f32[2,256]{1,0:T(2,128)} %param.15) | copy-start | bytes 6148
  37.2 120.8 %all-to-all-start = ((bf16[40,2,32768]{2,0,1:T(8,128)(2,1)}), bf16[40,2,32768]{2,0,1:T(8,128)(2,1)}, u32[]{:S(2)}, u32[]{:S(2)}) async-start(bf16[40,2,32768]{2,0,1:T(8,128)(2,1)} %bitcast.83), calls=%async_computation | async-start | bytes 10485760 | tf_op jit(solution)/shard_map/all_to_all | solution.py:98
  43.4 288.4 %all-reduce.5.cloned.1.call-start = ((), (), s32[]{:S(2)}) async-start(), calls=%async_computation.3 | async-start | bytes 262144 | tf_op jit(solution)/shard_map/psum | solution.py:107
Sparse Core Ops, SparseCore 0:
  32.1 122.9 all-reduce.2
  207.4 124.3 all-reduce.4
where the time goes:
time: 390 us; the launch traced here: 388 us
  waiting for transfers between devices  236 us (61%)
  matrix products  46.8 us (12%)
  local copies, waits for them, and re-layouts  46.5 us (12%)
  other arithmetic  28.8 us (7%)
  between operations  13.7 us (4%)
  blocking collectives  9.38 us (2%)
  starting transfers between devices  6.23 us (2%)
    psum x1, waiting for transfers between devices, on_device(): lax.psum(collect_prior(realization_vectors, measured_segment_index[batch_...  125 us
    psum x1, waiting for transfers between devices, on_device(): early_prior = lax.psum(padded, ('mem', 'state'))  112 us
    dot_general x16, matrix products, update_block(): lax.dot_general(increment, gain_matrix, (((1,), (1,)), ((), ())), preferr...  46.8 us
    reduce_sum x16, other arithmetic, update_block(): centred = (values - jnp.mean(values, axis=0)).astype(jnp.bfloat16)  19.4 us
    unnamed x15, local copies, waits for them, and re-layouts  14.9 us
    while x3, local copies, waits for them, and re-layouts, apply_batch(): lax.fori_loop(0, realization_vectors.shape[1] // BLK, advance, realizatio...  9.69 us
    all_to_all x1, blocking collectives, on_device(): lax.all_to_all(realization_vectors, 'mem', split_axis=0, concat_axis=1, t...  9.38 us
    gather x1, local copies, waits for them, and re-layouts, on_device(): jnp.take(background_ensemble, jnp.clip(column, 0, background_ensemble.sha...  8.65 us
  transfers between devices with their start and end apart: 3, of which 2 were waited for; matrix products, arithmetic and copies ran while one was open for 2% of the time, Pallas kernels for 0%

commit v1 on v0

v1 whole, which is shorter than its diff:
```python
import functools

import jax
import jax.numpy as jnp
from jax import lax
from jax.experimental import pallas as pl
from jax.experimental.pallas import tpu as pltpu
from jax.sharding import PartitionSpec as P

ENSEMBLE_COUNT = 80
SD = 32768
K = 256
B = 2
LB = 128
CHUNK = 2048
DEPTH = 128
BF = jnp.bfloat16
F32 = jnp.float32


def pick_kernel(slab_ref, seg_ref, place_ref, x_ref, out_ref):
    members, width = x_ref.shape
    base = slab_ref[0] * width
    lanes = lax.broadcasted_iota(jnp.int32, (members, LB), 1)
    for group in range(B * K // LB):
        batch, first = divmod(group * LB, K)

        def step(i, acc):
            column = seg_ref[batch, first + i] * SD + place_ref[batch, first + i] - base
            held = (column >= 0) & (column < width)
            column = jnp.clip(column, 0, width - 1)
            start = pl.multiple_of((column >> 7) * LB, LB)
            block = x_ref[:, pl.ds(start, LB)].astype(F32)
            turned = pltpu.roll(block, (i - (column & (LB - 1)) + LB) & (LB - 1), 1)
            return jnp.where(lanes == jnp.where(held, i, -1), turned, acc)

        acc = lax.fori_loop(0, LB, step, jnp.zeros((members, LB), F32), unroll=8)
        out_ref[:, group * LB : (group + 1) * LB] = acc.astype(out_ref.dtype)


def stats(prior, values, variances):
    centre = jnp.sum(prior, axis=0, keepdims=True) / ENSEMBLE_COUNT
    anomaly = prior - centre
    prior_var = jnp.sum(anomaly * anomaly, axis=0, keepdims=True) / (ENSEMBLE_COUNT - 1) + 1e-06
    post_var = 1.0 / (1.0 / prior_var + 1.0 / variances)
    post_mean = post_var * (centre / prior_var + values / variances)
    shrink = jnp.sqrt(post_var / prior_var)
    increment = (post_mean - centre + (shrink - 1.0) * anomaly).astype(BF)
    return increment, anomaly, 1.0 / ((ENSEMBLE_COUNT - 1) * prior_var)


def deep(values):
    rows, columns = values.shape
    return jnp.concatenate([values, jnp.zeros((DEPTH - rows, columns), F32)], axis=0)


def centred_of(values):
    return deep(values - jnp.sum(values, axis=0, keepdims=True) / ENSEMBLE_COUNT).astype(BF)


def members_last(anomaly):
    turned = jnp.transpose(deep(anomaly))
    return turned.astype(BF)


def dot(a, b):
    return jnp.dot(a, b, preferred_element_type=F32)


def update_kernel(
    slab_ref, seg_ref, place_ref, reading_ref, noise_ref, damp_ref, cutoff_ref,
    mine_ref, other_ref, x_ref, y_ref, out_ref, inc1, inc2, anom1, anom2, rows,
):
    step = pl.program_id(0)
    own = x_ref.shape[0]
    blocks = x_ref.shape[1] // LB

    @pl.when(step == 0)
    def _():
        prior = jnp.concatenate([mine_ref[...].astype(F32), other_ref[...].astype(F32)], axis=0)
        place = [(seg_ref[b : b + 1] * SD + place_ref[b : b + 1]) // LB for b in range(B)]
        place = [p.astype(F32) for p in place]
        reach = [1.0 / (cutoff_ref[b : b + 1].astype(F32) + 1.0) for b in range(B)]
        damp = [damp_ref[b : b + 1] for b in range(B)]
        first, a, scale = stats(prior[:, :K], reading_ref[0:1], noise_ref[0:1])
        anom1[...] = members_last(a)
        inc1[...] = first.astype(F32)
        side = jnp.concatenate([damp[0] * scale, place[0], reach[0], jnp.zeros((DEPTH - 3, K), F32)], axis=0)
        side = jnp.transpose(side)
        later = prior[:, K:]
        covariance = dot(anom1[...], centred_of(later))
        taper = jnp.maximum(0.0, 1.0 - jnp.abs(place[1] - side[:, 1:2]) * side[:, 2:3])
        gain = (side[:, 0:1] * taper * covariance).astype(BF)
        later = (later + dot(first, gain)).astype(BF).astype(F32)
        second, a, scale2 = stats(later, reading_ref[1:2], noise_ref[1:2])
        anom2[...] = members_last(a)
        inc2[...] = second.astype(F32)[:own]
        rows[...] = jnp.concatenate(
            [damp[0] * scale, place[0], reach[0], damp[1] * scale2, place[1], reach[1], jnp.zeros((2, K), F32)],
            axis=0,
        )

    base = (slab_ref[0] * pl.num_programs(0) + step) * blocks

    def scaled(increment, at, block):
        away = jnp.abs((base + block).astype(F32) - rows[at + 1 : at + 2])
        return increment * (rows[at : at + 1] * jnp.maximum(0.0, 1.0 - away * rows[at + 2 : at + 3]))

    left1, left2 = inc1[...], inc2[...]
    every = left1.shape[0]
    group = 8
    for low in range(0, blocks, group):
        some = range(low, low + group)
        t1 = dot(jnp.concatenate([scaled(left1, 0, b) for b in some], axis=0).astype(BF), anom1[...])
        t2 = dot(jnp.concatenate([scaled(left2, 3, b) for b in some], axis=0).astype(BF), anom2[...])
        for n, b in enumerate(some):
            at = slice(b * LB, (b + 1) * LB)
            values = jnp.concatenate([x_ref[:, at].astype(F32), y_ref[:, at].astype(F32)], axis=0)
            change = dot(t1[n * every : (n + 1) * every].astype(BF), centred_of(values))
            values = (values + change).astype(BF).astype(F32)
            change = dot(t2[n * own : (n + 1) * own].astype(BF), centred_of(values))
            out_ref[:, at] = (values[:own] + change).astype(BF)


def on_device(x, segment, place, readings, noise, damping, cutoff):
    members, width = x.shape
    slab = lax.axis_index("state").astype(jnp.int32).reshape(1)
    swap = [(0, 1), (1, 0)]
    y = lax.ppermute(x, "mem", swap)
    smem = pl.BlockSpec(memory_space=pltpu.SMEM)
    vmem = pl.BlockSpec(memory_space=pltpu.VMEM)
    mine = pl.pallas_call(
        pick_kernel,
        out_shape=jax.ShapeDtypeStruct((members, B * K), BF),
        in_specs=[smem, smem, smem, vmem],
        out_specs=vmem,
        compiler_params=pltpu.CompilerParams(vmem_limit_bytes=16 * 2**20),
        cost_estimate=pl.CostEstimate(flops=10**7, bytes_accessed=x.size * 2, transcendentals=0),
        name="pick",
    )(slab, segment, place, x)
    size = lax.axis_size("state")
    hop = 1
    while hop < size:
        mine = mine + lax.ppermute(mine, "state", [(i, i ^ hop) for i in range(size)])
        hop *= 2
    other = lax.ppermute(mine, "mem", swap)
    whole = lambda a: pl.BlockSpec(a.shape, lambda i: (0, 0))
    part = pl.BlockSpec((members, CHUNK), lambda i: (0, i))
    small = [segment, place, readings, noise, damping, cutoff, mine, other]
    return pl.pallas_call(
        update_kernel,
        grid=(width // CHUNK,),
        out_shape=jax.ShapeDtypeStruct(x.shape, x.dtype),
        in_specs=[smem] + [whole(a) for a in small] + [part, part],
        out_specs=part,
        scratch_shapes=[
            pltpu.VMEM((2 * members, K), F32),
            pltpu.VMEM((members, K), F32),
            pltpu.VMEM((K, DEPTH), BF),
            pltpu.VMEM((K, DEPTH), BF),
            pltpu.VMEM((8, K), F32),
        ],
        compiler_params=pltpu.CompilerParams(vmem_limit_bytes=32 * 2**20),
        cost_estimate=pl.CostEstimate(flops=width * 4 * 10**5, bytes_accessed=x.size * 6, transcendentals=0),
        name="update",
    )(slab, *small, x, y)


def solution(mesh):
    placed = (P("mem", "state"), P(), P(), P(), P(), P(), P())
    return jax.shard_map(
        on_device, mesh=mesh, in_specs=placed, out_specs=P("mem", "state"), check_vma=False
    )
```

time: 390 us -> 126 us (0.32)
  waiting for transfers between devices: 236 us -> 9.74 us
  Pallas kernels: 0 us -> 102 us
  matrix products: 46.8 us -> 0 us
  local copies, waits for them, and re-layouts: 46.5 us -> 3.87 us
  other arithmetic: 28.8 us -> 0.05 us
  between operations: 13.7 us -> 0.08 us
  blocking collectives: 9.38 us -> 0 us
  starting transfers between devices: 6.23 us -> 10.3 us
    psum x2 -> x0, waiting for transfers between devices: 236 us -> none  [the longest x1 125 us: on_device(): lax.psum(collect_prior(realization_vectors, measured_segment_index[batch_...]
    pallas_call x0 -> x2, Pallas kernels: none -> 102 us  [the longest x1 93.3 us: on_device(): pl.pallas_call(update_kernel, grid=(width // CHUNK,), out_shape=jax.Shape...]
    dot_general x16 -> x0, matrix products: 46.8 us -> none  [update_block(): lax.dot_general(increment, gain_matrix, (((1,), (1,)), ((), ())), preferr...]
    reduce_sum x20 -> x0, other arithmetic: 23.3 us -> none  [the longest x16 19.4 us: update_block(): centred = (values - jnp.mean(values, axis=0)).astype(jnp.bfloat16)]
    gather x2 -> x0, local copies, waits for them, and re-layouts: 13.8 us -> none  [the longest x1 8.65 us: on_device(): jnp.take(background_ensemble, jnp.clip(column, 0, background_ensemble.sha...]
    unnamed x15 -> x20, local copies, waits for them, and re-layouts: 14.9 us -> 3.87 us
    ppermute x0 -> x6, starting transfers between devices: none -> 10.3 us  [the longest x4 9.71 us: on_device(): lax.ppermute(mine, 'state', [(i, i ^ hop) for i in range(size)])]
    ppermute x0 -> x6, waiting for transfers between devices: none -> 9.74 us  [the longest x4 8.53 us: on_device(): lax.ppermute(mine, 'state', [(i, i ^ hop) for i in range(size)])]
  transfers between devices with their start and end apart: 3 -> 6, of which waited for: 2 -> 5; matrix products, arithmetic and copies ran while one was open for 2% -> 0% of each run, Pallas kernels for 0% -> 7%
where the time goes in v1:
time: 126 us
  Pallas kernels  102 us (81%)
  starting transfers between devices  10.3 us (8%)
  waiting for transfers between devices  9.74 us (8%)
  local copies, waits for them, and re-layouts  3.87 us (3%)
    pallas_call x1, Pallas kernels, on_device(): pl.pallas_call(update_kernel, grid=(width // CHUNK,), out_shape=jax.Shape...  93.3 us
    ppermute x4, starting transfers between devices, on_device(): lax.ppermute(mine, 'state', [(i, i ^ hop) for i in range(size)])  9.71 us
    ppermute x4, waiting for transfers between devices, on_device(): lax.ppermute(mine, 'state', [(i, i ^ hop) for i in range(size)])  8.53 us
    pallas_call x1, Pallas kernels, on_device(): pl.pallas_call(pick_kernel, out_shape=jax.ShapeDtypeStruct((members, B *...  8.52 us
    unnamed x20, local copies, waits for them, and re-layouts  3.87 us
  transfers between devices with their start and end apart: 6, of which 5 were waited for; matrix products, arithmetic and copies ran while one was open for 0% of the time, Pallas kernels for 7%

profile of v1, /device:TPU:0, one launch (start us, length us, event | category | flops | bytes accessed | tf_op | source)
XLA Modules:
  0.0 125.8 jit_solution(1592393585042727490)
XLA Ops:
  0.0 0.0 copy-start.5
  0.0 0.0 copy-start.3
  0.0 0.0 copy-start.6
  0.0 0.5 collective-permute-start.5
  0.5 0.0 copy-start
  0.5 2.5 %copy-done = bf16[40,65536]{1,0:T(8,128)(2,1)S(1)} copy-done((bf16[40,65536]{1,0:T(8,128)(2,1)S(1)}, bf16[40,65536]{1,0:T(8,128)(2,1)}, u32[]{:S(2)}) %copy-start) | copy-done | bytes 5242904
  3.0 0.0 copy-start.2
  3.0 0.7 copy-done.2
  3.7 0.0 copy-start.4
  3.7 0.7 copy-done.4
  4.4 0.0 copy-start.1
  4.4 0.0 copy-start.7
  4.4 0.0 copy-start.8
  4.4 0.0 copy-start.9
  4.4 8.5 %pick.1 = bf16[40,512]{1,0:T(8,128)(2,1)S(1)} custom-call(s32[1]{0:T(128)} %bitcast.slab_ref, s32[2,256]{1,0:T(2,128)S(1)} %copy-done.2, s32[2,256]{1,0:T(2,128)S(1)} %copy-done.4, bf16[40,65536]{1,0:T(8,128)(2,1)S(1)} %copy-done), custom_call_target="tpu_custom_call" | custom-call | flops 10000000 | bytes 5242880 | tf_op jit(solution)/shard_map/pick/pallas_call | solution.py:132
  12.9 2.6 %collective-permute-start = (bf16[40,512]{1,0:T(8,128)(2,1)S(1)}, bf16[40,512]{1,0:T(8,128)(2,1)S(1)}, u32[]{:S(2)}, u32[]{:S(2)}) collective-permute-start(bf16[40,512]{1,0:T(8,128)(2,1)S(1)} %pick.1), channel_id=1, source_target_pairs={{0,1},{1,0},{2,3},{3,2},{4,5},{5,4},{6,7},{7,6},{8,9},{9,8},{10,11... | collective-permute-start | bytes 122888 | tf_op jit(solution)/shard_map/ppermute | solution.py:144
  15.5 2.2 %collective-permute-done = bf16[40,512]{1,0:T(8,128)(2,1)S(1)} collective-permute-done((bf16[40,512]{1,0:T(8,128)(2,1)S(1)}, bf16[40,512]{1,0:T(8,128)(2,1)S(1)}, u32[]{:S(2)}, u32[]{:S(2)}) %collective-permute-start) | collective-permute-done | bytes 40992 | tf_op jit(solution)/shard_map/ppermute | solution.py:144
  17.7 1.9 %collective-permute-start.1 = (bf16[40,512]{1,0:T(8,128)(2,1)S(1)}, bf16[40,512]{1,0:T(8,128)(2,1)S(1)}, u32[]{:S(2)}, u32[]{:S(2)}) collective-permute-start(bf16[40,512]{1,0:T(8,128)(2,1)S(1)} %add.12), channel_id=1, source_target_pairs={{0,2},{1,3},{2,0},{3,1},{4,6},{5,7},{6,4},{7,5},{8,10},{9,11},{10,... | collective-permute-start | bytes 122888 | tf_op jit(solution)/shard_map/ppermute | solution.py:144
  19.6 2.2 %collective-permute-done.1 = bf16[40,512]{1,0:T(8,128)(2,1)S(1)} collective-permute-done((bf16[40,512]{1,0:T(8,128)(2,1)S(1)}, bf16[40,512]{1,0:T(8,128)(2,1)S(1)}, u32[]{:S(2)}, u32[]{:S(2)}) %collective-permute-start.1) | collective-permute-done | bytes 40992 | tf_op jit(solution)/shard_map/ppermute | solution.py:144
  21.8 1.9 %collective-permute-start.2 = (bf16[40,512]{1,0:T(8,128)(2,1)S(1)}, bf16[40,512]{1,0:T(8,128)(2,1)S(1)}, u32[]{:S(2)}, u32[]{:S(2)}) collective-permute-start(bf16[40,512]{1,0:T(8,128)(2,1)S(1)} %add.13), channel_id=1, source_target_pairs={{0,4},{1,5},{2,6},{3,7},{4,0},{5,1},{6,2},{7,3},{8,12},{9,13},{10,... | collective-permute-start | bytes 122888 | tf_op jit(solution)/shard_map/ppermute | solution.py:144
  23.7 2.1 %collective-permute-done.2 = bf16[40,512]{1,0:T(8,128)(2,1)S(1)} collective-permute-done((bf16[40,512]{1,0:T(8,128)(2,1)S(1)}, bf16[40,512]{1,0:T(8,128)(2,1)S(1)}, u32[]{:S(2)}, u32[]{:S(2)}) %collective-permute-start.2) | collective-permute-done | bytes 40992 | tf_op jit(solution)/shard_map/ppermute | solution.py:144
  25.9 3.3 %collective-permute-start.3 = (bf16[40,512]{1,0:T(8,128)(2,1)S(1)}, bf16[40,512]{1,0:T(8,128)(2,1)S(1)}, u32[]{:S(2)}, u32[]{:S(2)}) collective-permute-start(bf16[40,512]{1,0:T(8,128)(2,1)S(1)} %add.14), channel_id=1, source_target_pairs={{0,8},{1,9},{2,10},{3,11},{4,12},{5,13},{6,14},{7,15},{8,0},{9,1},... | collective-permute-start | bytes 122888 | tf_op jit(solution)/shard_map/ppermute | solution.py:144
  29.2 2.0 %collective-permute-done.3 = bf16[40,512]{1,0:T(8,128)(2,1)S(1)} collective-permute-done((bf16[40,512]{1,0:T(8,128)(2,1)S(1)}, bf16[40,512]{1,0:T(8,128)(2,1)S(1)}, u32[]{:S(2)}, u32[]{:S(2)}) %collective-permute-start.3) | collective-permute-done | bytes 40992 | tf_op jit(solution)/shard_map/ppermute | solution.py:144
  31.2 0.1 collective-permute-start.4
  31.3 1.2 collective-permute-done.4.other_ref
  32.5 0.0 collective-permute-done.5.y_ref
  32.5 0.0 copy-done.5
  32.5 0.0 copy-done.3
  32.5 0.0 copy-done.6
  32.5 0.0 copy-done.1
  32.5 0.0 copy-done.7
  32.5 0.0 copy-done.8
  32.6 0.0 copy-done.9
  32.6 93.3 %update.1 = bf16[40,65536]{1,0:T(8,128)(2,1)} custom-call(s32[1]{0:T(128)} %bitcast.slab_ref, s32[2,256]{1,0:T(2,128)S(1)} %copy-done.3, s32[2,256]{1,0:T(2,128)S(1)} %copy-done.5, f32[2,256]{1,0:T(2,128)S(1)} %copy-done.6, f32[2,256]{1,0:T(2,128)S(1)} %copy-done.7, f32[2,256]{1,0:T(2,128)S(1)} %copy-done.8, s32[2,256]{1,0:T(2,128)S(1)} %copy-done.9, ...), custom_call_target="tpu_custom_call" | custom-call | flops 26214400000 | bytes 15728640 | tf_op jit(solution)/shard_map/update/pallas_call | solution.py:150
  (4 shorter events, 0.1 us)
Async XLA Ops:
  0.0 32.5 %copy-start.5 = (s32[2,256]{1,0:T(2,128)S(1)}, s32[2,256]{1,0:T(2,128)}, u32[]{:S(2)}) copy-start(s32[2,256]{1,0:T(2,128)} %place_ref.3) | copy-start | bytes 6148
  0.0 32.5 %copy-start.3 = (s32[2,256]{1,0:T(2,128)S(1)}, s32[2,256]{1,0:T(2,128)}, u32[]{:S(2)}) copy-start(s32[2,256]{1,0:T(2,128)} %seg_ref.3) | copy-start | bytes 6148
  0.0 32.5 %copy-start.6 = (f32[2,256]{1,0:T(2,128)S(1)}, f32[2,256]{1,0:T(2,128)}, u32[]{:S(2)}) copy-start(f32[2,256]{1,0:T(2,128)} %reading_ref.1) | copy-start | bytes 6148
  0.0 32.5 %collective-permute-start.5 = (bf16[40,65536]{1,0:T(8,128)(2,1)}, bf16[40,65536]{1,0:T(8,128)(2,1)}, u32[]{:S(2)}, u32[]{:S(2)}) collective-permute-start(bf16[40,65536]{1,0:T(8,128)(2,1)} %x_ref.3), channel_id=1, source_target_pairs={{0,16},{16,0},{1,17},{17,1},{2,18},{18,2},{3,19},{19,3},{4,20},{20... | collective-permute-start | bytes 15728648 | tf_op jit(solution)/shard_map/ppermute | solution.py:129
  0.5 2.5 %copy-start = (bf16[40,65536]{1,0:T(8,128)(2,1)S(1)}, bf16[40,65536]{1,0:T(8,128)(2,1)}, u32[]{:S(2)}) copy-start(bf16[40,65536]{1,0:T(8,128)(2,1)} %x_ref.3) | copy-start | bytes 15728644
  3.0 0.7 copy-start.2
  3.7 0.7 copy-start.4
  4.4 28.2 %copy-start.1 = (bf16[40,65536]{1,0:T(8,128)(2,1)S(1)}, bf16[40,65536]{1,0:T(8,128)(2,1)}, u32[]{:S(2)}) copy-start(bf16[40,65536]{1,0:T(8,128)(2,1)} %x_ref.3) | copy-start | bytes 15728644
  4.4 28.2 %copy-start.7 = (f32[2,256]{1,0:T(2,128)S(1)}, f32[2,256]{1,0:T(2,128)}, u32[]{:S(2)}) copy-start(f32[2,256]{1,0:T(2,128)} %noise_ref.1) | copy-start | bytes 6148
  4.4 28.2 %copy-start.8 = (f32[2,256]{1,0:T(2,128)S(1)}, f32[2,256]{1,0:T(2,128)}, u32[]{:S(2)}) copy-start(f32[2,256]{1,0:T(2,128)} %damp_ref.1) | copy-start | bytes 6148
  4.4 28.2 %copy-start.9 = (s32[2,256]{1,0:T(2,128)S(1)}, s32[2,256]{1,0:T(2,128)}, u32[]{:S(2)}) copy-start(s32[2,256]{1,0:T(2,128)} %cutoff_ref.1) | copy-start | bytes 6148
  12.9 4.8 %collective-permute-start = (bf16[40,512]{1,0:T(8,128)(2,1)S(1)}, bf16[40,512]{1,0:T(8,128)(2,1)S(1)}, u32[]{:S(2)}, u32[]{:S(2)}) collective-permute-start(bf16[40,512]{1,0:T(8,128)(2,1)S(1)} %pick.1), channel_id=1, source_target_pairs={{0,1},{1,0},{2,3},{3,2},{4,5},{5,4},{6,7},{7,6},{8,9},{9,8},{10,11... | collective-permute-start | bytes 122888 | tf_op jit(solution)/shard_map/ppermute | solution.py:144
  17.7 4.1 %collective-permute-start.1 = (bf16[40,512]{1,0:T(8,128)(2,1)S(1)}, bf16[40,512]{1,0:T(8,128)(2,1)S(1)}, u32[]{:S(2)}, u32[]{:S(2)}) collective-permute-start(bf16[40,512]{1,0:T(8,128)(2,1)S(1)} %add.12), channel_id=1, source_target_pairs={{0,2},{1,3},{2,0},{3,1},{4,6},{5,7},{6,4},{7,5},{8,10},{9,11},{10,... | collective-permute-start | bytes 122888 | tf_op jit(solution)/shard_map/ppermute | solution.py:144
  21.8 4.1 %collective-permute-start.2 = (bf16[40,512]{1,0:T(8,128)(2,1)S(1)}, bf16[40,512]{1,0:T(8,128)(2,1)S(1)}, u32[]{:S(2)}, u32[]{:S(2)}) collective-permute-start(bf16[40,512]{1,0:T(8,128)(2,1)S(1)} %add.13), channel_id=1, source_target_pairs={{0,4},{1,5},{2,6},{3,7},{4,0},{5,1},{6,2},{7,3},{8,12},{9,13},{10,... | collective-permute-start | bytes 122888 | tf_op jit(solution)/shard_map/ppermute | solution.py:144
  25.9 5.3 %collective-permute-start.3 = (bf16[40,512]{1,0:T(8,128)(2,1)S(1)}, bf16[40,512]{1,0:T(8,128)(2,1)S(1)}, u32[]{:S(2)}, u32[]{:S(2)}) collective-permute-start(bf16[40,512]{1,0:T(8,128)(2,1)S(1)} %add.14), channel_id=1, source_target_pairs={{0,8},{1,9},{2,10},{3,11},{4,12},{5,13},{6,14},{7,15},{8,0},{9,1},... | collective-permute-start | bytes 122888 | tf_op jit(solution)/shard_map/ppermute | solution.py:144
  31.2 1.3 %collective-permute-start.4 = (bf16[40,512]{1,0:T(8,128)(2,1)S(1)}, bf16[40,512]{1,0:T(8,128)(2,1)S(1)}, u32[]{:S(2)}, u32[]{:S(2)}) collective-permute-start(bf16[40,512]{1,0:T(8,128)(2,1)S(1)} %add.15.mine_ref), channel_id=1, source_target_pairs={{0,16},{16,0},{1,17},{17,1},{2,18},{18,2},{3,19},{19,3},{4,20},{20... | collective-permute-start | bytes 122888 | tf_op jit(solution)/shard_map/ppermute | solution.py:146

commit v2 on v1

--- a/solution.py
+++ b/solution.py
@@ -12,7 +12,8 @@
 K = 256
 B = 2
 LB = 128
-CHUNK = 2048
+CHUNK = 4096
+GROUP = 16
 DEPTH = 128
 BF = jnp.bfloat16
 F32 = jnp.float32
@@ -69,7 +70,7 @@
 
 def update_kernel(
     slab_ref, seg_ref, place_ref, reading_ref, noise_ref, damp_ref, cutoff_ref,
-    mine_ref, other_ref, x_ref, y_ref, out_ref, inc1, inc2, anom1, anom2, rows,
+    mine_ref, other_ref, x_ref, y_ref, out_ref, inc1, inc2, anom1, right, rows,
 ):
     step = pl.program_id(0)
     own = x_ref.shape[0]
@@ -84,7 +85,8 @@
         damp = [damp_ref[b : b + 1] for b in range(B)]
         first, a, scale = stats(prior[:, :K], reading_ref[0:1], noise_ref[0:1])
         anom1[...] = members_last(a)
-        inc1[...] = first.astype(F32)
+        increment = first.astype(F32)
+        inc1[...] = increment[:own]
         side = jnp.concatenate([damp[0] * scale, place[0], reach[0], jnp.zeros((DEPTH - 3, K), F32)], axis=0)
         side = jnp.transpose(side)
         later = prior[:, K:]
@@ -93,7 +95,9 @@
         gain = (side[:, 0:1] * taper * covariance).astype(BF)
         later = (later + dot(first, gain)).astype(BF).astype(F32)
         second, a, scale2 = stats(later, reading_ref[1:2], noise_ref[1:2])
-        anom2[...] = members_last(a)
+        anom2 = members_last(a)
+        right[:, :K] = dot(anom2, centred_of(increment)).astype(BF)
+        right[:, K:] = anom2
         inc2[...] = second.astype(F32)[:own]
         rows[...] = jnp.concatenate(
             [damp[0] * scale, place[0], reach[0], damp[1] * scale2, place[1], reach[1], jnp.zeros((2, K), F32)],
@@ -102,24 +106,33 @@
 
     base = (slab_ref[0] * pl.num_programs(0) + step) * blocks
 
-    def scaled(increment, at, block):
+    def weight(at, block):
         away = jnp.abs((base + block).astype(F32) - rows[at + 1 : at + 2])
-        return increment * (rows[at : at + 1] * jnp.maximum(0.0, 1.0 - away * rows[at + 2 : at + 3]))
+        return rows[at : at + 1] * jnp.maximum(0.0, 1.0 - away * rows[at + 2 : at + 3])
 
     left1, left2 = inc1[...], inc2[...]
-    every = left1.shape[0]
-    group = 8
-    for low in range(0, blocks, group):
-        some = range(low, low + group)
-        t1 = dot(jnp.concatenate([scaled(left1, 0, b) for b in some], axis=0).astype(BF), anom1[...])
-        t2 = dot(jnp.concatenate([scaled(left2, 3, b) for b in some], axis=0).astype(BF), anom2[...])
-        for n, b in enumerate(some):
-            at = slice(b * LB, (b + 1) * LB)
-            values = jnp.concatenate([x_ref[:, at].astype(F32), y_ref[:, at].astype(F32)], axis=0)
-            change = dot(t1[n * every : (n + 1) * every].astype(BF), centred_of(values))
-            values = (values + change).astype(BF).astype(F32)
-            change = dot(t2[n * own : (n + 1) * own].astype(BF), centred_of(values))
-            out_ref[:, at] = (values[:own] + change).astype(BF)
+    none = jnp.zeros((own, DEPTH), F32)
+    for low in range(0, blocks, GROUP):
+        some = range(low, low + GROUP)
+        both = dot(jnp.concatenate([left2 * weight(3, b) for b in some], axis=0).astype(BF), right[...])
+        first = [
+            (left1 + both[n * own : (n + 1) * own, :K]) * weight(0, b) for n, b in enumerate(some)
+        ]
+        matrix = both[:, K:] + dot(jnp.concatenate(first, axis=0).astype(BF), anom1[...])
+        for n in range(0, GROUP, 2):
+            pair = [slice((low + n + i) * LB, (low + n + i + 1) * LB) for i in (0, 1)]
+            mine = [x_ref[:, at].astype(F32) for at in pair]
+            deeps = [
+                centred_of(jnp.concatenate([m, y_ref[:, at].astype(F32)], axis=0))
+                for m, at in zip(mine, pair)
+            ]
+            upper = jnp.concatenate([matrix[n * own : (n + 1) * own], none], axis=1)
+            lower = jnp.concatenate([none, matrix[(n + 1) * own : (n + 2) * own]], axis=1)
+            change = dot(
+                jnp.concatenate([upper, lower], axis=0).astype(BF), jnp.concatenate(deeps, axis=0)
+            )
+            for i in (0, 1):
+                out_ref[:, pair[i]] = (mine[i] + change[i * own : (i + 1) * own]).astype(BF)
 
 
 def on_device(x, segment, place, readings, noise, damping, cutoff):
@@ -154,10 +167,10 @@
         in_specs=[smem] + [whole(a) for a in small] + [part, part],
         out_specs=part,
         scratch_shapes=[
-            pltpu.VMEM((2 * members, K), F32),
+            pltpu.VMEM((members, K), F32),
             pltpu.VMEM((members, K), F32),
             pltpu.VMEM((K, DEPTH), BF),
-            pltpu.VMEM((K, DEPTH), BF),
+            pltpu.VMEM((K, K + DEPTH), BF),
             pltpu.VMEM((8, K), F32),
         ],
         compiler_params=pltpu.CompilerParams(vmem_limit_bytes=32 * 2**20),

time: 126 us -> 54.1 us (0.43)
  Pallas kernels: 102 us -> 29.8 us
    pallas_call x1, Pallas kernels: 93.3 us -> 21.3 us  [on_device(): pl.pallas_call(update_kernel, grid=(width // CHUNK,), out_shape=jax.Shape...]
  transfers between devices with their start and end apart: 6 -> 6, of which waited for: 5 -> 5; matrix products, arithmetic and copies ran while one was open for 0% -> 0% of each run, Pallas kernels for 7% -> 16%
where the time goes in v2:
time: 54.1 us; the launch traced here: 53.9 us
  Pallas kernels  29.8 us (55%)
  starting transfers between devices  10.3 us (19%)
  waiting for transfers between devices  9.74 us (18%)
  local copies, waits for them, and re-layouts  3.87 us (7%)
    pallas_call x1, Pallas kernels, on_device(): pl.pallas_call(update_kernel, grid=(width // CHUNK,), out_shape=jax.Shape...  21.3 us
    ppermute x4, starting transfers between devices, on_device(): lax.ppermute(mine, 'state', [(i, i ^ hop) for i in range(size)])  9.71 us
    ppermute x4, waiting for transfers between devices, on_device(): lax.ppermute(mine, 'state', [(i, i ^ hop) for i in range(size)])  8.53 us
    pallas_call x1, Pallas kernels, on_device(): pl.pallas_call(pick_kernel, out_shape=jax.ShapeDtypeStruct((members, B *...  8.52 us
    unnamed x20, local copies, waits for them, and re-layouts  3.87 us
    ppermute x1, waiting for transfers between devices, on_device(): other = lax.ppermute(mine, 'mem', swap)  1.21 us
  transfers between devices with their start and end apart: 6, of which 5 were waited for; matrix products, arithmetic and copies ran while one was open for 0% of the time, Pallas kernels for 16%

profile of v2, /device:TPU:0, one launch (start us, length us, event | category | flops | bytes accessed | tf_op | source)
XLA Modules:
  0.0 53.9 jit_solution(16071089721189500506)
XLA Ops:
  0.0 0.0 copy-start.5
  0.0 0.0 copy-start.3
  0.0 0.0 copy-start.6
  0.0 0.5 collective-permute-start.5
  0.5 0.0 copy-start
  0.5 2.5 %copy-done = bf16[40,65536]{1,0:T(8,128)(2,1)S(1)} copy-done((bf16[40,65536]{1,0:T(8,128)(2,1)S(1)}, bf16[40,65536]{1,0:T(8,128)(2,1)}, u32[]{:S(2)}) %copy-start) | copy-done | bytes 5242904
  3.0 0.0 copy-start.2
  3.0 0.7 %copy-done.2 = s32[2,256]{1,0:T(2,128)S(1)} copy-done((s32[2,256]{1,0:T(2,128)S(1)}, s32[2,256]{1,0:T(2,128)}, u32[]{:S(2)}) %copy-start.2) | copy-done | bytes 2072
  3.7 0.0 copy-start.4
  3.7 0.7 %copy-done.4 = s32[2,256]{1,0:T(2,128)S(1)} copy-done((s32[2,256]{1,0:T(2,128)S(1)}, s32[2,256]{1,0:T(2,128)}, u32[]{:S(2)}) %copy-start.4) | copy-done | bytes 2072
  4.4 0.0 copy-start.1
  4.4 0.0 copy-start.7
  4.4 0.0 copy-start.8
  4.4 0.0 copy-start.9
  4.4 8.5 %pick.1 = bf16[40,512]{1,0:T(8,128)(2,1)S(1)} custom-call(s32[1]{0:T(128)} %bitcast.slab_ref, s32[2,256]{1,0:T(2,128)S(1)} %copy-done.2, s32[2,256]{1,0:T(2,128)S(1)} %copy-done.4, bf16[40,65536]{1,0:T(8,128)(2,1)S(1)} %copy-done), custom_call_target="tpu_custom_call" | custom-call | flops 10000000 | bytes 5242880 | tf_op jit(solution)/shard_map/pick/pallas_call | solution.py:145
  12.9 2.6 %collective-permute-start = (bf16[40,512]{1,0:T(8,128)(2,1)S(1)}, bf16[40,512]{1,0:T(8,128)(2,1)S(1)}, u32[]{:S(2)}, u32[]{:S(2)}) collective-permute-start(bf16[40,512]{1,0:T(8,128)(2,1)S(1)} %pick.1), channel_id=1, source_target_pairs={{0,1},{1,0},{2,3},{3,2},{4,5},{5,4},{6,7},{7,6},{8,9},{9,8},{10,11... | collective-permute-start | bytes 122888 | tf_op jit(solution)/shard_map/ppermute | solution.py:157
  15.5 2.2 %collective-permute-done = bf16[40,512]{1,0:T(8,128)(2,1)S(1)} collective-permute-done((bf16[40,512]{1,0:T(8,128)(2,1)S(1)}, bf16[40,512]{1,0:T(8,128)(2,1)S(1)}, u32[]{:S(2)}, u32[]{:S(2)}) %collective-permute-start) | collective-permute-done | bytes 40992 | tf_op jit(solution)/shard_map/ppermute | solution.py:157
  17.7 1.9 %collective-permute-start.1 = (bf16[40,512]{1,0:T(8,128)(2,1)S(1)}, bf16[40,512]{1,0:T(8,128)(2,1)S(1)}, u32[]{:S(2)}, u32[]{:S(2)}) collective-permute-start(bf16[40,512]{1,0:T(8,128)(2,1)S(1)} %add.12), channel_id=1, source_target_pairs={{0,2},{1,3},{2,0},{3,1},{4,6},{5,7},{6,4},{7,5},{8,10},{9,11},{10,... | collective-permute-start | bytes 122888 | tf_op jit(solution)/shard_map/ppermute | solution.py:157
  19.6 2.2 %collective-permute-done.1 = bf16[40,512]{1,0:T(8,128)(2,1)S(1)} collective-permute-done((bf16[40,512]{1,0:T(8,128)(2,1)S(1)}, bf16[40,512]{1,0:T(8,128)(2,1)S(1)}, u32[]{:S(2)}, u32[]{:S(2)}) %collective-permute-start.1) | collective-permute-done | bytes 40992 | tf_op jit(solution)/shard_map/ppermute | solution.py:157
  21.8 1.9 %collective-permute-start.2 = (bf16[40,512]{1,0:T(8,128)(2,1)S(1)}, bf16[40,512]{1,0:T(8,128)(2,1)S(1)}, u32[]{:S(2)}, u32[]{:S(2)}) collective-permute-start(bf16[40,512]{1,0:T(8,128)(2,1)S(1)} %add.13), channel_id=1, source_target_pairs={{0,4},{1,5},{2,6},{3,7},{4,0},{5,1},{6,2},{7,3},{8,12},{9,13},{10,... | collective-permute-start | bytes 122888 | tf_op jit(solution)/shard_map/ppermute | solution.py:157
  23.7 2.1 %collective-permute-done.2 = bf16[40,512]{1,0:T(8,128)(2,1)S(1)} collective-permute-done((bf16[40,512]{1,0:T(8,128)(2,1)S(1)}, bf16[40,512]{1,0:T(8,128)(2,1)S(1)}, u32[]{:S(2)}, u32[]{:S(2)}) %collective-permute-start.2) | collective-permute-done | bytes 40992 | tf_op jit(solution)/shard_map/ppermute | solution.py:157
  25.9 3.3 %collective-permute-start.3 = (bf16[40,512]{1,0:T(8,128)(2,1)S(1)}, bf16[40,512]{1,0:T(8,128)(2,1)S(1)}, u32[]{:S(2)}, u32[]{:S(2)}) collective-permute-start(bf16[40,512]{1,0:T(8,128)(2,1)S(1)} %add.14), channel_id=1, source_target_pairs={{0,8},{1,9},{2,10},{3,11},{4,12},{5,13},{6,14},{7,15},{8,0},{9,1},... | collective-permute-start | bytes 122888 | tf_op jit(solution)/shard_map/ppermute | solution.py:157
  29.2 2.0 %collective-permute-done.3 = bf16[40,512]{1,0:T(8,128)(2,1)S(1)} collective-permute-done((bf16[40,512]{1,0:T(8,128)(2,1)S(1)}, bf16[40,512]{1,0:T(8,128)(2,1)S(1)}, u32[]{:S(2)}, u32[]{:S(2)}) %collective-permute-start.3) | collective-permute-done | bytes 40992 | tf_op jit(solution)/shard_map/ppermute | solution.py:157
  31.2 0.1 collective-permute-start.4
  31.3 1.2 %collective-permute-done.4.other_ref = bf16[40,512]{1,0:T(8,128)(2,1)S(1)} collective-permute-done((bf16[40,512]{1,0:T(8,128)(2,1)S(1)}, bf16[40,512]{1,0:T(8,128)(2,1)S(1)}, u32[]{:S(2)}, u32[]{:S(2)}) %collective-permute-start.4) | collective-permute-done | bytes 40992 | tf_op jit(solution)/shard_map/ppermute | solution.py:159
  32.5 0.0 collective-permute-done.5.y_ref
  32.5 0.0 copy-done.5
  32.5 0.0 copy-done.3
  32.5 0.0 copy-done.6
  32.5 0.0 copy-done.1
  32.5 0.0 copy-done.7
  32.5 0.0 copy-done.8
  32.6 0.0 copy-done.9
  32.6 21.3 %update.1 = bf16[40,65536]{1,0:T(8,128)(2,1)} custom-call(s32[1]{0:T(128)} %bitcast.slab_ref, s32[2,256]{1,0:T(2,128)S(1)} %copy-done.3, s32[2,256]{1,0:T(2,128)S(1)} %copy-done.5, f32[2,256]{1,0:T(2,128)S(1)} %copy-done.6, f32[2,256]{1,0:T(2,128)S(1)} %copy-done.7, f32[2,256]{1,0:T(2,128)S(1)} %copy-done.8, s32[2,256]{1,0:T(2,128)S(1)} %copy-done.9, ...), custom_call_target="tpu_custom_call" | custom-call | flops 26214400000 | bytes 15728640 | tf_op jit(solution)/shard_map/update/pallas_call | solution.py:163
  (4 shorter events, 0.1 us)
Async XLA Ops:
  0.0 32.5 %copy-start.5 = (s32[2,256]{1,0:T(2,128)S(1)}, s32[2,256]{1,0:T(2,128)}, u32[]{:S(2)}) copy-start(s32[2,256]{1,0:T(2,128)} %place_ref.3) | copy-start | bytes 6148
  0.0 32.5 %copy-start.3 = (s32[2,256]{1,0:T(2,128)S(1)}, s32[2,256]{1,0:T(2,128)}, u32[]{:S(2)}) copy-start(s32[2,256]{1,0:T(2,128)} %seg_ref.3) | copy-start | bytes 6148
  0.0 32.5 %copy-start.6 = (f32[2,256]{1,0:T(2,128)S(1)}, f32[2,256]{1,0:T(2,128)}, u32[]{:S(2)}) copy-start(f32[2,256]{1,0:T(2,128)} %reading_ref.1) | copy-start | bytes 6148
  0.0 32.5 %collective-permute-start.5 = (bf16[40,65536]{1,0:T(8,128)(2,1)}, bf16[40,65536]{1,0:T(8,128)(2,1)}, u32[]{:S(2)}, u32[]{:S(2)}) collective-permute-start(bf16[40,65536]{1,0:T(8,128)(2,1)} %x_ref.3), channel_id=1, source_target_pairs={{0,16},{16,0},{1,17},{17,1},{2,18},{18,2},{3,19},{19,3},{4,20},{20... | collective-permute-start | bytes 15728648 | tf_op jit(solution)/shard_map/ppermute | solution.py:142
  0.5 2.5 %copy-start = (bf16[40,65536]{1,0:T(8,128)(2,1)S(1)}, bf16[40,65536]{1,0:T(8,128)(2,1)}, u32[]{:S(2)}) copy-start(bf16[40,65536]{1,0:T(8,128)(2,1)} %x_ref.3) | copy-start | bytes 15728644
  3.0 0.7 %copy-start.2 = (s32[2,256]{1,0:T(2,128)S(1)}, s32[2,256]{1,0:T(2,128)}, u32[]{:S(2)}) copy-start(s32[2,256]{1,0:T(2,128)} %seg_ref.3) | copy-start | bytes 6148
  3.7 0.7 %copy-start.4 = (s32[2,256]{1,0:T(2,128)S(1)}, s32[2,256]{1,0:T(2,128)}, u32[]{:S(2)}) copy-start(s32[2,256]{1,0:T(2,128)} %place_ref.3) | copy-start | bytes 6148
  4.4 28.2 %copy-start.1 = (bf16[40,65536]{1,0:T(8,128)(2,1)S(1)}, bf16[40,65536]{1,0:T(8,128)(2,1)}, u32[]{:S(2)}) copy-start(bf16[40,65536]{1,0:T(8,128)(2,1)} %x_ref.3) | copy-start | bytes 15728644
  4.4 28.2 %copy-start.7 = (f32[2,256]{1,0:T(2,128)S(1)}, f32[2,256]{1,0:T(2,128)}, u32[]{:S(2)}) copy-start(f32[2,256]{1,0:T(2,128)} %noise_ref.1) | copy-start | bytes 6148
  4.4 28.2 %copy-start.8 = (f32[2,256]{1,0:T(2,128)S(1)}, f32[2,256]{1,0:T(2,128)}, u32[]{:S(2)}) copy-start(f32[2,256]{1,0:T(2,128)} %damp_ref.1) | copy-start | bytes 6148
  4.4 28.2 %copy-start.9 = (s32[2,256]{1,0:T(2,128)S(1)}, s32[2,256]{1,0:T(2,128)}, u32[]{:S(2)}) copy-start(s32[2,256]{1,0:T(2,128)} %cutoff_ref.1) | copy-start | bytes 6148
  12.9 4.8 %collective-permute-start = (bf16[40,512]{1,0:T(8,128)(2,1)S(1)}, bf16[40,512]{1,0:T(8,128)(2,1)S(1)}, u32[]{:S(2)}, u32[]{:S(2)}) collective-permute-start(bf16[40,512]{1,0:T(8,128)(2,1)S(1)} %pick.1), channel_id=1, source_target_pairs={{0,1},{1,0},{2,3},{3,2},{4,5},{5,4},{6,7},{7,6},{8,9},{9,8},{10,11... | collective-permute-start | bytes 122888 | tf_op jit(solution)/shard_map/ppermute | solution.py:157
  17.7 4.1 %collective-permute-start.1 = (bf16[40,512]{1,0:T(8,128)(2,1)S(1)}, bf16[40,512]{1,0:T(8,128)(2,1)S(1)}, u32[]{:S(2)}, u32[]{:S(2)}) collective-permute-start(bf16[40,512]{1,0:T(8,128)(2,1)S(1)} %add.12), channel_id=1, source_target_pairs={{0,2},{1,3},{2,0},{3,1},{4,6},{5,7},{6,4},{7,5},{8,10},{9,11},{10,... | collective-permute-start | bytes 122888 | tf_op jit(solution)/shard_map/ppermute | solution.py:157
  21.8 4.1 %collective-permute-start.2 = (bf16[40,512]{1,0:T(8,128)(2,1)S(1)}, bf16[40,512]{1,0:T(8,128)(2,1)S(1)}, u32[]{:S(2)}, u32[]{:S(2)}) collective-permute-start(bf16[40,512]{1,0:T(8,128)(2,1)S(1)} %add.13), channel_id=1, source_target_pairs={{0,4},{1,5},{2,6},{3,7},{4,0},{5,1},{6,2},{7,3},{8,12},{9,13},{10,... | collective-permute-start | bytes 122888 | tf_op jit(solution)/shard_map/ppermute | solution.py:157
  25.9 5.3 %collective-permute-start.3 = (bf16[40,512]{1,0:T(8,128)(2,1)S(1)}, bf16[40,512]{1,0:T(8,128)(2,1)S(1)}, u32[]{:S(2)}, u32[]{:S(2)}) collective-permute-start(bf16[40,512]{1,0:T(8,128)(2,1)S(1)} %add.14), channel_id=1, source_target_pairs={{0,8},{1,9},{2,10},{3,11},{4,12},{5,13},{6,14},{7,15},{8,0},{9,1},... | collective-permute-start | bytes 122888 | tf_op jit(solution)/shard_map/ppermute | solution.py:157
  31.2 1.3 %collective-permute-start.4 = (bf16[40,512]{1,0:T(8,128)(2,1)S(1)}, bf16[40,512]{1,0:T(8,128)(2,1)S(1)}, u32[]{:S(2)}, u32[]{:S(2)}) collective-permute-start(bf16[40,512]{1,0:T(8,128)(2,1)S(1)} %add.15.mine_ref), channel_id=1, source_target_pairs={{0,16},{16,0},{1,17},{17,1},{2,18},{18,2},{3,19},{19,3},{4,20},{20... | collective-permute-start | bytes 122888 | tf_op jit(solution)/shard_map/ppermute | solution.py:159

commit v3 on v2

--- a/solution.py
+++ b/solution.py
@@ -17,6 +17,7 @@
 DEPTH = 128
 BF = jnp.bfloat16
 F32 = jnp.float32
+MESH = pl.DeviceIdType.MESH
 
 
 def pick_kernel(slab_ref, seg_ref, place_ref, x_ref, out_ref):
@@ -36,7 +37,60 @@
             return jnp.where(lanes == jnp.where(held, i, -1), turned, acc)
 
         acc = lax.fori_loop(0, LB, step, jnp.zeros((members, LB), F32), unroll=8)
+        acc = jnp.concatenate([acc, jnp.zeros((out_ref.shape[0] - members, LB), F32)], axis=0)
         out_ref[:, group * LB : (group + 1) * LB] = acc.astype(out_ref.dtype)
+
+
+def share_kernel(radices, own_ref, mine_ref, other_ref, sums, slots, send_sem, recv_sem, swap_sem):
+    me = lax.axis_index("state")
+    sibling = {"mem": 1 - lax.axis_index("mem")}
+    partners, stride = [], 1
+    for radix in radices:
+        digit = (me // stride) % radix
+        partners.append(
+            [{"state": me + ((digit + r) % radix - digit) * stride} for r in range(1, radix)]
+        )
+        stride *= radix
+    barrier = pltpu.get_barrier_semaphore()
+    every = [p for stage in partners for p in stage] + [sibling]
+    for partner in every:
+        pl.semaphore_signal(barrier, inc=1, device_id=partner, device_id_type=MESH)
+    pl.semaphore_wait(barrier, len(every))
+
+    for stage, group in enumerate(partners):
+        source = own_ref if stage == 0 else sums.at[stage - 1]
+        copies = [
+            pltpu.make_async_remote_copy(
+                src_ref=source,
+                dst_ref=slots.at[stage, r],
+                send_sem=send_sem.at[stage, r],
+                recv_sem=recv_sem.at[stage, r],
+                device_id=partner,
+                device_id_type=MESH,
+            )
+            for r, partner in enumerate(group)
+        ]
+        for copy in copies:
+            copy.start()
+        total = source[...].astype(F32)
+        for copy in copies:
+            copy.wait()
+        for r in range(len(group)):
+            total = total + slots[stage, r].astype(F32)
+        sums[stage] = total.astype(BF)
+    last = sums.at[len(partners) - 1]
+    copy = pltpu.make_async_remote_copy(
+        src_ref=last,
+        dst_ref=slots.at[len(partners), 0],
+        send_sem=swap_sem.at[0],
+        recv_sem=swap_sem.at[1],
+        device_id=sibling,
+        device_id_type=MESH,
+    )
+    copy.start()
+    mine_ref[...] = last[...]
+    copy.wait()
+    other_ref[...] = slots[len(partners), 0]
 
 
 def stats(prior, values, variances):
@@ -78,7 +132,9 @@
 
     @pl.when(step == 0)
     def _():
-        prior = jnp.concatenate([mine_ref[...].astype(F32), other_ref[...].astype(F32)], axis=0)
+        prior = jnp.concatenate(
+            [mine_ref[...].astype(F32)[:own], other_ref[...].astype(F32)[:own]], axis=0
+        )
         place = [(seg_ref[b : b + 1] * SD + place_ref[b : b + 1]) // LB for b in range(B)]
         place = [p.astype(F32) for p in place]
         reach = [1.0 / (cutoff_ref[b : b + 1].astype(F32) + 1.0) for b in range(B)]
@@ -144,19 +200,37 @@
     vmem = pl.BlockSpec(memory_space=pltpu.VMEM)
     mine = pl.pallas_call(
         pick_kernel,
-        out_shape=jax.ShapeDtypeStruct((members, B * K), BF),
+        out_shape=jax.ShapeDtypeStruct((-(-members // 16) * 16, B * K), BF),
         in_specs=[smem, smem, smem, vmem],
         out_specs=vmem,
         compiler_params=pltpu.CompilerParams(vmem_limit_bytes=16 * 2**20),
         cost_estimate=pl.CostEstimate(flops=10**7, bytes_accessed=x.size * 2, transcendentals=0),
         name="pick",
     )(slab, segment, place, x)
-    size = lax.axis_size("state")
-    hop = 1
-    while hop < size:
-        mine = mine + lax.ppermute(mine, "state", [(i, i ^ hop) for i in range(size)])
-        hop *= 2
-    other = lax.ppermute(mine, "mem", swap)
+    size, radices = lax.axis_size("state"), []
+    while size > 1:
+        radices.append(4 if size % 4 == 0 else size)
+        size //= radices[-1]
+    stages, most = len(radices), max(radices) - 1
+    shared = jax.ShapeDtypeStruct(mine.shape, BF)
+    mine, other = pl.pallas_call(
+        functools.partial(share_kernel, radices),
+        out_shape=[shared, shared],
+        in_specs=[vmem],
+        out_specs=[vmem, vmem],
+        scratch_shapes=[
+            pltpu.VMEM((stages,) + mine.shape, BF),
+            pltpu.VMEM((stages + 1, most) + mine.shape, BF),
+            pltpu.SemaphoreType.DMA((stages, most)),
+            pltpu.SemaphoreType.DMA((stages, most)),
+            pltpu.SemaphoreType.DMA((2,)),
+        ],
+        compiler_params=pltpu.CompilerParams(
+            collective_id=0, has_side_effects=True, vmem_limit_bytes=8 * 2**20
+        ),
+        cost_estimate=pl.CostEstimate(flops=10**6, bytes_accessed=10**6, transcendentals=0),
+        name="share",
+    )(mine)
     whole = lambda a: pl.BlockSpec(a.shape, lambda i: (0, 0))
     part = pl.BlockSpec((members, CHUNK), lambda i: (0, i))
     small = [segment, place, readings, noise, damping, cutoff, mine, other]

time: 54.1 us -> 49.9 us (0.922)
  Pallas kernels: 29.8 us -> 45.2 us
  starting transfers between devices: 10.3 us -> 0.52 us
  waiting for transfers between devices: 9.74 us -> 0.01 us
    pallas_call x1 -> x2, Pallas kernels: 8.52 us -> 23.9 us  [the longest x1 15.4 us: on_device(): pl.pallas_call(functools.partial(share_kernel, radices), out_shape=[share...]
    ppermute x5 -> x0, starting transfers between devices: 9.78 us -> none  [the longest x4 9.71 us: on_device(): lax.ppermute(mine, 'state', [(i, i ^ hop) for i in range(size)])]
    ppermute x5 -> x0, waiting for transfers between devices: 9.74 us -> none  [the longest x4 8.53 us: on_device(): lax.ppermute(mine, 'state', [(i, i ^ hop) for i in range(size)])]
  transfers between devices with their start and end apart: 6 -> 1, of which waited for: 5 -> 0; matrix products, arithmetic and copies ran while one was open for 0% -> 0% of each run, Pallas kernels for 16% -> 48%
where the time goes in v3:
time: 49.9 us; the launch traced here: 49.7 us
  Pallas kernels  45.2 us (91%)
  local copies, waits for them, and re-layouts  3.87 us (8%)
  starting transfers between devices  0.52 us (1%)
    pallas_call x1, Pallas kernels, on_device(): pl.pallas_call(update_kernel, grid=(width // CHUNK,), out_shape=jax.Shape...  21.3 us
    pallas_call x1, Pallas kernels, on_device(): pl.pallas_call(functools.partial(share_kernel, radices), out_shape=[share...  15.4 us
    pallas_call x1, Pallas kernels, on_device(): pl.pallas_call(pick_kernel, out_shape=jax.ShapeDtypeStruct((-(-members //...  8.52 us
    unnamed x20, local copies, waits for them, and re-layouts  3.87 us
  transfers between devices with their start and end apart: 1, of which 0 were waited for; matrix products, arithmetic and copies ran while one was open for 0% of the time, Pallas kernels for 48%

profile of v3, /device:TPU:0, one launch (start us, length us, event | category | flops | bytes accessed | tf_op | source)
XLA Modules:
  0.0 49.7 jit_solution(12682258269508076121)
XLA Ops:
  0.0 0.0 copy-start.5
  0.0 0.0 copy-start.3
  0.0 0.0 copy-start.6
  0.0 0.5 %collective-permute-start = (bf16[40,65536]{1,0:T(8,128)(2,1)}, bf16[40,65536]{1,0:T(8,128)(2,1)}, u32[]{:S(2)}, u32[]{:S(2)}) collective-permute-start(bf16[40,65536]{1,0:T(8,128)(2,1)} %x_ref.3), channel_id=1, source_target_pairs={{0,16},{16,0},{1,17},{17,1},{2,18},{18,2},{3,19},{19,3},{4,20},{20... | collective-permute-start | bytes 15728648 | tf_op jit(solution)/shard_map/ppermute | solution.py:198
  0.5 0.0 copy-start
  0.5 2.5 %copy-done = bf16[40,65536]{1,0:T(8,128)(2,1)S(1)} copy-done((bf16[40,65536]{1,0:T(8,128)(2,1)S(1)}, bf16[40,65536]{1,0:T(8,128)(2,1)}, u32[]{:S(2)}) %copy-start) | copy-done | bytes 5242904
  3.0 0.0 copy-start.2
  3.0 0.7 %copy-done.2 = s32[2,256]{1,0:T(2,128)S(1)} copy-done((s32[2,256]{1,0:T(2,128)S(1)}, s32[2,256]{1,0:T(2,128)}, u32[]{:S(2)}) %copy-start.2) | copy-done | bytes 2072
  3.7 0.0 copy-start.4
  3.7 0.7 %copy-done.4 = s32[2,256]{1,0:T(2,128)S(1)} copy-done((s32[2,256]{1,0:T(2,128)S(1)}, s32[2,256]{1,0:T(2,128)}, u32[]{:S(2)}) %copy-start.4) | copy-done | bytes 2072
  4.4 0.0 copy-start.1
  4.4 0.0 copy-start.7
  4.4 0.0 copy-start.8
  4.4 0.0 copy-start.9
  4.4 8.5 %pick.1.own_ref = bf16[48,512]{1,0:T(8,128)(2,1)S(1)} custom-call(s32[1]{0:T(128)} %bitcast.slab_ref, s32[2,256]{1,0:T(2,128)S(1)} %copy-done.2, s32[2,256]{1,0:T(2,128)S(1)} %copy-done.4, bf16[40,65536]{1,0:T(8,128)(2,1)S(1)} %copy-done), custom_call_target="tpu_custom_call" | custom-call | flops 10000000 | bytes 5242880 | tf_op jit(solution)/shard_map/pick/pallas_call | solution.py:201
  12.9 15.4 %share.1 = (bf16[48,512]{1,0:T(8,128)(2,1)S(1)}, bf16[48,512]{1,0:T(8,128)(2,1)S(1)}) custom-call(bf16[48,512]{1,0:T(8,128)(2,1)S(1)} %pick.1.own_ref), custom_call_target="tpu_custom_call" | custom-call | flops 1000000 | bytes 1000000 | tf_op jit(solution)/shard_map/share/pallas_call | solution.py:216
  28.3 0.0 collective-permute-done.y_ref
  28.3 0.0 copy-done.5
  28.3 0.0 copy-done.3
  28.3 0.0 copy-done.6
  28.3 0.0 copy-done.1
  28.3 0.0 copy-done.7
  28.3 0.0 copy-done.8
  28.3 0.0 copy-done.9
  28.4 21.3 %update.1 = bf16[40,65536]{1,0:T(8,128)(2,1)} custom-call(s32[1]{0:T(128)} %bitcast.slab_ref, s32[2,256]{1,0:T(2,128)S(1)} %copy-done.3, s32[2,256]{1,0:T(2,128)S(1)} %copy-done.5, f32[2,256]{1,0:T(2,128)S(1)} %copy-done.6, f32[2,256]{1,0:T(2,128)S(1)} %copy-done.7, f32[2,256]{1,0:T(2,128)S(1)} %copy-done.8, s32[2,256]{1,0:T(2,128)S(1)} %copy-done.9, ...), custom_call_target="tpu_custom_call" | custom-call | flops 26214400000 | bytes 15728640 | tf_op jit(solution)/shard_map/update/pallas_call | solution.py:237
Async XLA Ops:
  0.0 28.3 %copy-start.5 = (s32[2,256]{1,0:T(2,128)S(1)}, s32[2,256]{1,0:T(2,128)}, u32[]{:S(2)}) copy-start(s32[2,256]{1,0:T(2,128)} %place_ref.3) | copy-start | bytes 6148
  0.0 28.3 %copy-start.3 = (s32[2,256]{1,0:T(2,128)S(1)}, s32[2,256]{1,0:T(2,128)}, u32[]{:S(2)}) copy-start(s32[2,256]{1,0:T(2,128)} %seg_ref.3) | copy-start | bytes 6148
  0.0 28.3 %copy-start.6 = (f32[2,256]{1,0:T(2,128)S(1)}, f32[2,256]{1,0:T(2,128)}, u32[]{:S(2)}) copy-start(f32[2,256]{1,0:T(2,128)} %reading_ref.1) | copy-start | bytes 6148
  0.0 28.3 %collective-permute-start = (bf16[40,65536]{1,0:T(8,128)(2,1)}, bf16[40,65536]{1,0:T(8,128)(2,1)}, u32[]{:S(2)}, u32[]{:S(2)}) collective-permute-start(bf16[40,65536]{1,0:T(8,128)(2,1)} %x_ref.3), channel_id=1, source_target_pairs={{0,16},{16,0},{1,17},{17,1},{2,18},{18,2},{3,19},{19,3},{4,20},{20... | collective-permute-start | bytes 15728648 | tf_op jit(solution)/shard_map/ppermute | solution.py:198
  0.5 2.5 %copy-start = (bf16[40,65536]{1,0:T(8,128)(2,1)S(1)}, bf16[40,65536]{1,0:T(8,128)(2,1)}, u32[]{:S(2)}) copy-start(bf16[40,65536]{1,0:T(8,128)(2,1)} %x_ref.3) | copy-start | bytes 15728644
  3.0 0.7 %copy-start.2 = (s32[2,256]{1,0:T(2,128)S(1)}, s32[2,256]{1,0:T(2,128)}, u32[]{:S(2)}) copy-start(s32[2,256]{1,0:T(2,128)} %seg_ref.3) | copy-start | bytes 6148
  3.7 0.7 %copy-start.4 = (s32[2,256]{1,0:T(2,128)S(1)}, s32[2,256]{1,0:T(2,128)}, u32[]{:S(2)}) copy-start(s32[2,256]{1,0:T(2,128)} %place_ref.3) | copy-start | bytes 6148
  4.4 23.9 %copy-start.1 = (bf16[40,65536]{1,0:T(8,128)(2,1)S(1)}, bf16[40,65536]{1,0:T(8,128)(2,1)}, u32[]{:S(2)}) copy-start(bf16[40,65536]{1,0:T(8,128)(2,1)} %x_ref.3) | copy-start | bytes 15728644
  4.4 23.9 %copy-start.7 = (f32[2,256]{1,0:T(2,128)S(1)}, f32[2,256]{1,0:T(2,128)}, u32[]{:S(2)}) copy-start(f32[2,256]{1,0:T(2,128)} %noise_ref.1) | copy-start | bytes 6148
  4.4 23.9 %copy-start.8 = (f32[2,256]{1,0:T(2,128)S(1)}, f32[2,256]{1,0:T(2,128)}, u32[]{:S(2)}) copy-start(f32[2,256]{1,0:T(2,128)} %damp_ref.1) | copy-start | bytes 6148
  4.4 24.0 %copy-start.9 = (s32[2,256]{1,0:T(2,128)S(1)}, s32[2,256]{1,0:T(2,128)}, u32[]{:S(2)}) copy-start(s32[2,256]{1,0:T(2,128)} %cutoff_ref.1) | copy-start | bytes 6148

commit v4 on v3

--- a/solution.py
+++ b/solution.py
@@ -36,7 +36,7 @@
             turned = pltpu.roll(block, (i - (column & (LB - 1)) + LB) & (LB - 1), 1)
             return jnp.where(lanes == jnp.where(held, i, -1), turned, acc)
 
-        acc = lax.fori_loop(0, LB, step, jnp.zeros((members, LB), F32), unroll=8)
+        acc = lax.fori_loop(0, LB, step, jnp.zeros((members, LB), F32), unroll=32)
         acc = jnp.concatenate([acc, jnp.zeros((out_ref.shape[0] - members, LB), F32)], axis=0)
         out_ref[:, group * LB : (group + 1) * LB] = acc.astype(out_ref.dtype)
 

time: 49.9 us -> 47.4 us (0.950)
  Pallas kernels: 45.2 us -> 42.7 us
    pallas_call x1, Pallas kernels: 8.52 us -> 6.02 us  [on_device(): pl.pallas_call(pick_kernel, out_shape=jax.ShapeDtypeStruct((-(-members //...]
  transfers between devices with their start and end apart: 1 -> 1, of which waited for: 0 -> 0; matrix products, arithmetic and copies ran while one was open for 0% -> 0% of each run, Pallas kernels for 48% -> 45%
where the time goes in v4:
time: 47.4 us; the launch traced here: 47.2 us
  Pallas kernels  42.7 us (90%)
  local copies, waits for them, and re-layouts  3.87 us (8%)
  starting transfers between devices  0.52 us (1%)
    pallas_call x1, Pallas kernels, on_device(): pl.pallas_call(update_kernel, grid=(width // CHUNK,), out_shape=jax.Shape...  21.3 us
    pallas_call x1, Pallas kernels, on_device(): pl.pallas_call(functools.partial(share_kernel, radices), out_shape=[share...  15.4 us
    pallas_call x1, Pallas kernels, on_device(): pl.pallas_call(pick_kernel, out_shape=jax.ShapeDtypeStruct((-(-members //...  6.02 us
    unnamed x20, local copies, waits for them, and re-layouts  3.87 us
  transfers between devices with their start and end apart: 1, of which 0 were waited for; matrix products, arithmetic and copies ran while one was open for 0% of the time, Pallas kernels for 45%

profile of v4, /device:TPU:0, one launch (start us, length us, event | category | flops | bytes accessed | tf_op | source)
XLA Modules:
  0.0 47.2 jit_solution(11848192671522615513)
XLA Ops:
  0.0 0.0 copy-start.5
  0.0 0.0 copy-start.3
  0.0 0.0 copy-start.6
  0.0 0.5 %collective-permute-start = (bf16[40,65536]{1,0:T(8,128)(2,1)}, bf16[40,65536]{1,0:T(8,128)(2,1)}, u32[]{:S(2)}, u32[]{:S(2)}) collective-permute-start(bf16[40,65536]{1,0:T(8,128)(2,1)} %x_ref.3), channel_id=1, source_target_pairs={{0,16},{16,0},{1,17},{17,1},{2,18},{18,2},{3,19},{19,3},{4,20},{20... | collective-permute-start | bytes 15728648 | tf_op jit(solution)/shard_map/ppermute | solution.py:198
  0.5 0.0 copy-start
  0.5 2.5 %copy-done = bf16[40,65536]{1,0:T(8,128)(2,1)S(1)} copy-done((bf16[40,65536]{1,0:T(8,128)(2,1)S(1)}, bf16[40,65536]{1,0:T(8,128)(2,1)}, u32[]{:S(2)}) %copy-start) | copy-done | bytes 5242904
  3.0 0.0 copy-start.2
  3.0 0.7 %copy-done.2 = s32[2,256]{1,0:T(2,128)S(1)} copy-done((s32[2,256]{1,0:T(2,128)S(1)}, s32[2,256]{1,0:T(2,128)}, u32[]{:S(2)}) %copy-start.2) | copy-done | bytes 2072
  3.7 0.0 copy-start.4
  3.7 0.7 %copy-done.4 = s32[2,256]{1,0:T(2,128)S(1)} copy-done((s32[2,256]{1,0:T(2,128)S(1)}, s32[2,256]{1,0:T(2,128)}, u32[]{:S(2)}) %copy-start.4) | copy-done | bytes 2072
  4.4 0.0 copy-start.1
  4.4 0.0 copy-start.7
  4.4 0.0 copy-start.8
  4.4 0.0 copy-start.9
  4.4 6.0 %pick.1.own_ref = bf16[48,512]{1,0:T(8,128)(2,1)S(1)} custom-call(s32[1]{0:T(128)} %bitcast.slab_ref, s32[2,256]{1,0:T(2,128)S(1)} %copy-done.2, s32[2,256]{1,0:T(2,128)S(1)} %copy-done.4, bf16[40,65536]{1,0:T(8,128)(2,1)S(1)} %copy-done), custom_call_target="tpu_custom_call" | custom-call | flops 10000000 | bytes 5242880 | tf_op jit(solution)/shard_map/pick/pallas_call | solution.py:201
  10.4 15.4 %share.1 = (bf16[48,512]{1,0:T(8,128)(2,1)S(1)}, bf16[48,512]{1,0:T(8,128)(2,1)S(1)}) custom-call(bf16[48,512]{1,0:T(8,128)(2,1)S(1)} %pick.1.own_ref), custom_call_target="tpu_custom_call" | custom-call | flops 1000000 | bytes 1000000 | tf_op jit(solution)/shard_map/share/pallas_call | solution.py:216
  25.8 0.0 collective-permute-done.y_ref
  25.8 0.0 copy-done.5
  25.8 0.0 copy-done.3
  25.8 0.0 copy-done.6
  25.8 0.0 copy-done.1
  25.8 0.0 copy-done.7
  25.8 0.0 copy-done.8
  25.8 0.0 copy-done.9
  25.9 21.3 %update.1 = bf16[40,65536]{1,0:T(8,128)(2,1)} custom-call(s32[1]{0:T(128)} %bitcast.slab_ref, s32[2,256]{1,0:T(2,128)S(1)} %copy-done.3, s32[2,256]{1,0:T(2,128)S(1)} %copy-done.5, f32[2,256]{1,0:T(2,128)S(1)} %copy-done.6, f32[2,256]{1,0:T(2,128)S(1)} %copy-done.7, f32[2,256]{1,0:T(2,128)S(1)} %copy-done.8, s32[2,256]{1,0:T(2,128)S(1)} %copy-done.9, ...), custom_call_target="tpu_custom_call" | custom-call | flops 26214400000 | bytes 15728640 | tf_op jit(solution)/shard_map/update/pallas_call | solution.py:237
Async XLA Ops:
  0.0 25.8 %copy-start.5 = (s32[2,256]{1,0:T(2,128)S(1)}, s32[2,256]{1,0:T(2,128)}, u32[]{:S(2)}) copy-start(s32[2,256]{1,0:T(2,128)} %place_ref.3) | copy-start | bytes 6148
  0.0 25.8 %copy-start.3 = (s32[2,256]{1,0:T(2,128)S(1)}, s32[2,256]{1,0:T(2,128)}, u32[]{:S(2)}) copy-start(s32[2,256]{1,0:T(2,128)} %seg_ref.3) | copy-start | bytes 6148
  0.0 25.8 %copy-start.6 = (f32[2,256]{1,0:T(2,128)S(1)}, f32[2,256]{1,0:T(2,128)}, u32[]{:S(2)}) copy-start(f32[2,256]{1,0:T(2,128)} %reading_ref.1) | copy-start | bytes 6148
  0.0 25.8 %collective-permute-start = (bf16[40,65536]{1,0:T(8,128)(2,1)}, bf16[40,65536]{1,0:T(8,128)(2,1)}, u32[]{:S(2)}, u32[]{:S(2)}) collective-permute-start(bf16[40,65536]{1,0:T(8,128)(2,1)} %x_ref.3), channel_id=1, source_target_pairs={{0,16},{16,0},{1,17},{17,1},{2,18},{18,2},{3,19},{19,3},{4,20},{20... | collective-permute-start | bytes 15728648 | tf_op jit(solution)/shard_map/ppermute | solution.py:198
  0.5 2.5 %copy-start = (bf16[40,65536]{1,0:T(8,128)(2,1)S(1)}, bf16[40,65536]{1,0:T(8,128)(2,1)}, u32[]{:S(2)}) copy-start(bf16[40,65536]{1,0:T(8,128)(2,1)} %x_ref.3) | copy-start | bytes 15728644
  3.0 0.7 %copy-start.2 = (s32[2,256]{1,0:T(2,128)S(1)}, s32[2,256]{1,0:T(2,128)}, u32[]{:S(2)}) copy-start(s32[2,256]{1,0:T(2,128)} %seg_ref.3) | copy-start | bytes 6148
  3.7 0.7 %copy-start.4 = (s32[2,256]{1,0:T(2,128)S(1)}, s32[2,256]{1,0:T(2,128)}, u32[]{:S(2)}) copy-start(s32[2,256]{1,0:T(2,128)} %place_ref.3) | copy-start | bytes 6148
  4.4 21.4 %copy-start.1 = (bf16[40,65536]{1,0:T(8,128)(2,1)S(1)}, bf16[40,65536]{1,0:T(8,128)(2,1)}, u32[]{:S(2)}) copy-start(bf16[40,65536]{1,0:T(8,128)(2,1)} %x_ref.3) | copy-start | bytes 15728644
  4.4 21.4 %copy-start.7 = (f32[2,256]{1,0:T(2,128)S(1)}, f32[2,256]{1,0:T(2,128)}, u32[]{:S(2)}) copy-start(f32[2,256]{1,0:T(2,128)} %noise_ref.1) | copy-start | bytes 6148
  4.4 21.5 %copy-start.8 = (f32[2,256]{1,0:T(2,128)S(1)}, f32[2,256]{1,0:T(2,128)}, u32[]{:S(2)}) copy-start(f32[2,256]{1,0:T(2,128)} %damp_ref.1) | copy-start | bytes 6148
  4.4 21.5 %copy-start.9 = (s32[2,256]{1,0:T(2,128)S(1)}, s32[2,256]{1,0:T(2,128)}, u32[]{:S(2)}) copy-start(s32[2,256]{1,0:T(2,128)} %cutoff_ref.1) | copy-start | bytes 6148
